TPU v7x, 128 devices: a whole 4x4x4 slice. The times are simulated.
128 devices in a mesh: node: 16 (over y, x), local: 8 (over z, core).
Axes of the slice: x: 4, y: 4, z: 4, core: 2. Of those that a mesh axis runs over, the one named last changes fastest.
Arguments:
- moe_in: bfloat16 [2048, 3584], P(('node', 'local')), may hold values from -6 to 6
- route_ids: int32 [2048, 8], P(('node', 'local')), may hold values from 0 to 127, as said below
- route_weights: float32 [2048, 8], P(('node', 'local')), may hold values from 0.05 to 0.6
- w_gate: bfloat16 [128, 3584, 1024], P(('node', 'local')), may hold values from -0.09375 to 0.09375
- w_up: bfloat16 [128, 3584, 1024], P(('node', 'local')), may hold values from -0.09375 to 0.09375
- w_down: bfloat16 [128, 1024, 3584], P(('node', 'local')), may hold values from -0.1875 to 0.1875
- queries: bfloat16 [128, 128, 576], P(('node', 'local')), may hold values from -70 to 70
- cache_latent: bfloat16 [128, 2048, 512], P(('node', 'local')), may hold values from -12 to 12
- cache_rope: bfloat16 [128, 64, 2048], P(('node', 'local')), may hold values from -2 to 2
- lengths: int32 [128], P(('node', 'local')), may hold values from 256 to 2048, as said below
Outputs:
- moe_out: bfloat16 [2048, 3584], P(('node', 'local'))
- attn_out: bfloat16 [128, 128, 512], P(('node', 'local'))
Inputs may be any that keep to these rules, and one draw needn't show every extreme that they name: `route_ids`: each row names 8 different experts, 2 in each of 4 different node groups; expert e lies in node group e // 8 and is held by the device of flat index e (node major). Within the rows of one device (aligned blocks of 16 rows) no node group is used by more than 8 rows and no expert is named by more than 2 rows; in every such block some node group is used by exactly 8 rows and each of its experts is named by exactly 2 rows. `lengths`: at least one row has all 2048 slots filled.
All inputs are finite; a program needn't handle non-finite values.
Results may differ from a plain program's by a relative error of at most 0.012.
Values may be sent and summed in bfloat16 or wider, within the bound.
No kernel may reach another device: no remote copies, remote signals or barrier semaphores. Data moves between devices by JAX's collectives and lax.ppermute only.
A program may use at most 128 MiB of HBM per device.

v0:
```python
import jax
import jax.numpy as jnp
from jax import lax
from jax.sharding import PartitionSpec as P

score_scale = 192.0 ** (-0.5)


def expert_block(block, gate_one, up_one, down_one):
    model_width = block.shape[-1]
    rows_flat = block.reshape(-1, model_width)
    gate_act = jnp.dot(rows_flat, gate_one, preferred_element_type=jnp.float32)
    up_act = jnp.dot(rows_flat, up_one, preferred_element_type=jnp.float32)
    hidden_act = (jax.nn.silu(gate_act) * up_act).astype(jnp.bfloat16)
    result = jnp.dot(hidden_act, down_one, preferred_element_type=jnp.float32).astype(jnp.bfloat16)
    return result.reshape(block.shape)


def attention(queries, cache_latent, cache_rope, lengths):
    kv_width = cache_latent.shape[-1]
    scores = jnp.einsum(
        "rhc,rkc->rhk", queries[:, :, :kv_width], cache_latent, preferred_element_type=jnp.float32
    )
    scores = (
        scores
        + jnp.einsum(
            "rhc,rck->rhk", queries[:, :, kv_width:], cache_rope, preferred_element_type=jnp.float32
        )
    ) * score_scale
    positions = jnp.arange(cache_latent.shape[1], dtype=jnp.int32)
    scores = jnp.where(positions[None, None, :] < lengths[:, None, None], scores, -jnp.inf)
    peak = jnp.max(scores, axis=-1, keepdims=True)
    weights = jnp.exp(scores - peak)
    probs = (weights / jnp.sum(weights, axis=-1, keepdims=True)).astype(jnp.bfloat16)
    return jnp.einsum(
        "rhk,rkc->rhc", probs, cache_latent, preferred_element_type=jnp.float32
    ).astype(jnp.bfloat16)


def local(
    moe_in,
    route_ids,
    route_weights,
    w_gate,
    w_up,
    w_down,
    queries,
    cache_latent,
    cache_rope,
    lengths,
):
    attn_out = attention(queries, cache_latent, cache_rope, lengths)
    node_count = lax.axis_size("node")
    local_count = lax.axis_size("local")
    expert_count = node_count * local_count
    row_count, model_width = moe_in.shape
    top_count = route_ids.shape[1]
    capacity = 2 * row_count * top_count // expert_count
    gate_one = w_gate[0]
    up_one = w_up[0]
    down_one = w_down[0]
    row_index = jnp.broadcast_to(jnp.arange(row_count, dtype=jnp.int32)[:, None], route_ids.shape)
    padded = jnp.concatenate([moe_in, jnp.zeros((1, model_width), moe_in.dtype)], axis=0)
    expert_hits = (
        route_ids[:, :, None] == jnp.arange(expert_count, dtype=jnp.int32)[None, None, :]
    ).astype(jnp.int32)
    present = jnp.sum(expert_hits, axis=1, dtype=jnp.int32)
    earlier = jnp.cumsum(present, axis=0, dtype=jnp.int32) - present
    rank_of = jnp.sum(expert_hits * earlier[:, None, :], axis=-1, dtype=jnp.int32)
    slot_of = route_ids * capacity + rank_of
    table = (
        jnp.full((expert_count * capacity,), row_count, jnp.int32)
        .at[slot_of.reshape(-1)]
        .set(row_index.reshape(-1))
    )
    outgoing = padded[table].reshape(expert_count, capacity, model_width)
    result = expert_block(
        lax.all_to_all(outgoing, ("node", "local"), split_axis=0, concat_axis=0, tiled=True),
        gate_one,
        up_one,
        down_one,
    )
    returned = lax.all_to_all(result, ("node", "local"), split_axis=0, concat_axis=0, tiled=True)
    picked = returned.reshape(expert_count * capacity, model_width)[slot_of]
    total = jnp.einsum("rk,rkd->rd", route_weights, picked.astype(jnp.float32))
    moe_out = total.astype(jnp.bfloat16)
    return (moe_out, attn_out)


def solution(mesh):
    placed = (
        P(("node", "local"), None),
        P(("node", "local"), None),
        P(("node", "local"), None),
        P(("node", "local"), None, None),
        P(("node", "local"), None, None),
        P(("node", "local"), None, None),
        P(("node", "local"), None, None),
        P(("node", "local"), None, None),
        P(("node", "local"), None, None),
        P(("node", "local")),
    )
    return jax.shard_map(
        local,
        mesh=mesh,
        in_specs=placed,
        out_specs=(P(("node", "local"), None), P(("node", "local"), None, None)),
        check_vma=False,
    )
```

profile of v0, /device:TPU:1, one launch (start us, length us, event | category | flops | bytes accessed | tf_op | source)
XLA Modules:
  0.0 121.6 jit_solution(14893655284962925092)
XLA Ops:
  0.6 0.0 copy-start
  0.6 0.9 copy.18
  1.6 0.1 convert_reduce_fusion
  1.7 0.4 select_reduce_fusion
  2.1 0.1 reshape.106
  2.2 0.1 reshape.136
  2.3 1.0 scatter_custom_fusion
  3.3 0.9 concatenate.3
  4.2 2.9 %gather_fusion = bf16[256,3584]{1,0:T(8,128)(2,1)} fusion(bf16[17,3584]{1,0:T(8,128)(2,1)S(1)} %concatenate.3, s32[1024]{0:T(1024)S(1)} %pad_clamp_fusion.1), kind=kCustom, calls=%fused_computation | custom fusion | bytes 3671040 | tf_op jit(solution)/shard_map/gather | solution.py:76
  7.2 4.8 %reshape.108 = bf16[128,2,3584]{2,1,0:T(2,128)(2,1)} reshape(bf16[256,3584]{1,0:T(8,128)(2,1)} %gather_fusion) | data formatting | bytes 3670016 | tf_op jit(solution)/shard_map/reshape | solution.py:76
  12.0 39.1 %all_to_all.10 = bf16[128,2,3584]{2,1,0:T(2,128)(2,1)} all-to-all(bf16[128,2,3584]{2,1,0:T(2,128)(2,1)} %reshape.108), channel_id=1, replica_groups=mesh['node'=16,'local'=8] {'node','local'}, dimensions={0} | all-to-all | bytes 3670016 | tf_op jit(solution)/shard_map/all_to_all | solution.py:78
  51.1 5.0 %reshape.109 = bf16[256,3584]{1,0:T(8,128)(2,1)} reshape(bf16[128,2,3584]{2,1,0:T(2,128)(2,1)} %all_to_all.10) | data formatting | bytes 3670016 | tf_op jit(solution)/shard_map/reshape | solution.py:11
  56.0 6.7 %fusion.4 = f32[256,1024]{1,0:T(8,128)} fusion(bf16[256,3584]{1,0:T(8,128)(2,1)} %reshape.109, bf16[1,3584,1024]{2,1,0:T(8,128)(2,1)} %param.13), kind=kOutput, calls=%fused_computation.7 | convolution fusion | flops 1879048192 | bytes 10223616 | tf_op jit(solution)/shard_map/dot_general | solution.py:12
  62.7 11.2 %fusion.6 = bf16[256,3584]{1,0:T(8,128)(2,1)} fusion(bf16[1,1024,3584]{2,1,0:T(8,128)(2,1)} %param.15, bf16[256,3584]{1,0:T(8,128)(2,1)} %reshape.109, bf16[1,3584,1024]{2,1,0:T(8,128)(2,1)} %param.14, f32[256,1024]{1,0:T(8,128)} %fusion.4), kind=kOutput, calls=%fused_computation.9 | convolution fusion | flops 3760586752 | bytes 19398656 | tf_op jit(solution)/shard_map/dot_general | solution.py:15
  73.9 4.8 %reshape.110 = bf16[128,2,3584]{2,1,0:T(2,128)(2,1)} reshape(bf16[256,3584]{1,0:T(8,128)(2,1)} %fusion.6) | data formatting | bytes 3670016 | tf_op jit(solution)/shard_map/reshape | solution.py:16
  78.7 5.8 %all-to-all-start.1 = ((bf16[128,2,3584]{2,1,0:T(2,128)(2,1)}), bf16[128,2,3584]{2,1,0:T(2,128)(2,1)}, u32[]{:S(2)}, u32[]{:S(2)}) async-start(bf16[128,2,3584]{2,1,0:T(2,128)(2,1)} %reshape.110), calls=%async_computation.1 | async-start | bytes 3670016 | tf_op jit(solution)/shard_map/all_to_all | solution.py:83
  84.5 0.0 copy-start.1
  84.5 0.1 reshape.126
  84.6 0.0 copy-done.3
  84.6 0.1 copy.20
  85.4 0.0 copy-done
  85.4 0.0 copy-done.2
  85.4 0.8 fusion.13
  86.2 0.0 copy-done.1
  86.3 0.4 fusion.44
  86.7 0.3 fusion.27
  87.0 1.2 fusion.24
  88.1 23.7 %all-to-all-done.1 = bf16[128,2,3584]{2,1,0:T(2,128)(2,1)} async-done(((bf16[128,2,3584]{2,1,0:T(2,128)(2,1)}), bf16[128,2,3584]{2,1,0:T(2,128)(2,1)}, u32[]{:S(2)}, u32[]{:S(2)}) %all-to-all-start.1) | async-done | bytes 1835040 | tf_op jit(solution)/shard_map/all_to_all | solution.py:83
  111.8 4.9 %reshape.111 = bf16[256,3584]{1,0:T(8,128)(2,1)} reshape(bf16[128,2,3584]{2,1,0:T(2,128)(2,1)} %all-to-all-done.1) | data formatting | bytes 3670016 | tf_op jit(solution)/shard_map/reshape | solution.py:84
  116.7 3.8 %gather_fusion.1 = bf16[128,3584]{1,0:T(8,128)(2,1)S(1)} fusion(bf16[256,3584]{1,0:T(8,128)(2,1)} %reshape.111, s32[1024]{0:T(1024)S(1)} %pad_clamp_fusion), kind=kCustom, calls=%fused_computation.1 | custom fusion | bytes 1835520 | tf_op jit(solution)/shard_map/gather | solution.py:84
  120.5 0.4 fusion.28
  120.9 0.7 copy.23
  (11 shorter events, 0.1 us)
Async XLA Ops:
  0.6 84.8 %copy-start = (bf16[1,2048,512]{2,1,0:T(8,128)(2,1)S(1)}, bf16[1,2048,512]{2,1,0:T(8,128)(2,1)}, u32[]{:S(2)}) copy-start(bf16[1,2048,512]{2,1,0:T(8,128)(2,1)} %param.17) | copy-start | bytes 6291460
  78.7 5.9 %copy-start.3 = (f32[16,8]{0,1:T(8,128)S(1)}, f32[16,8]{0,1:T(8,128)}, u32[]{:S(2)}) copy-start(f32[16,8]{0,1:T(8,128)} %param.12) | copy-start | bytes 1540
  78.7 6.7 %copy-start.2 = (bf16[1,128,576]{1,2,0:T(8,128)(2,1)S(1)}, bf16[1,128,576]{1,2,0:T(8,128)(2,1)}, u32[]{:S(2)}) copy-start(bf16[1,128,576]{1,2,0:T(8,128)(2,1)} %param.16) | copy-start | bytes 442372
  78.7 33.1 %all-to-all-start.1 = ((bf16[128,2,3584]{2,1,0:T(2,128)(2,1)}), bf16[128,2,3584]{2,1,0:T(2,128)(2,1)}, u32[]{:S(2)}, u32[]{:S(2)}) async-start(bf16[128,2,3584]{2,1,0:T(2,128)(2,1)} %reshape.110), calls=%async_computation.1 | async-start | bytes 3670016 | tf_op jit(solution)/shard_map/all_to_all | solution.py:83
  84.5 1.7 %copy-start.1 = (bf16[1,64,2048]{2,1,0:T(8,128)(2,1)S(1)}, bf16[1,64,2048]{2,1,0:T(8,128)(2,1)}, u32[]{:S(2)}) copy-start(bf16[1,64,2048]{2,1,0:T(8,128)(2,1)} %param.18) | copy-start | bytes 786436
where the time goes:
time: 122 us
  blocking collectives  39.1 us (32%)
  local copies, waits for them, and re-layouts  29.9 us (25%)
  waiting for transfers between devices  23.7 us (19%)
  matrix products  20.7 us (17%)
  starting transfers between devices  5.83 us (5%)
  between operations  1.45 us (1%)
    all_to_all x1, blocking collectives, local(): lax.all_to_all(outgoing, ('node', 'local'), split_axis=0, concat_axis=0,...  39.1 us
    all_to_all x1, waiting for transfers between devices, local(): lax.all_to_all(result, ('node', 'local'), split_axis=0, concat_axis=0, ti...  23.7 us
    dot_general x1, matrix products, expert_block(): jnp.dot(hidden_act, down_one, preferred_element_type=jnp.float32)  11.2 us
    dot_general x1, matrix products, expert_block(): gate_act = jnp.dot(rows_flat, gate_one, preferred_element_type=jnp.float32)  6.66 us
    all_to_all x1, starting transfers between devices, local(): lax.all_to_all(result, ('node', 'local'), split_axis=0, concat_axis=0, ti...  5.83 us
    reshape x1, local copies, waits for them, and re-layouts, expert_block(): rows_flat = block.reshape(-1, model_width)  4.95 us
    reshape x1, local copies, waits for them, and re-layouts, local(): picked = returned.reshape(expert_count * capacity, model_width)[slot_of]  4.91 us
    reshape x1, local copies, waits for them, and re-layouts, local(): outgoing = padded[table].reshape(expert_count, capacity, model_width)  4.79 us
  transfers between devices with their start and end apart: 1, of which 1 were waited for; matrix products, arithmetic and copies ran while one was open for 2% of the time, Pallas kernels for 0%

commit v1 on v0

v1 whole, which is shorter than its diff:
```python
import functools
import jax
import jax.numpy as jnp
from jax import lax
from jax.experimental import pallas as pl
from jax.experimental.pallas import tpu as pltpu
from jax.sharding import PartitionSpec as P

f32, bf16 = jnp.float32, jnp.bfloat16
score_scale = 192.0 ** (-0.5)
axes = ("node", "local")
SLOTS = 2
QUARTERS = 4
LANE = 128
PER = SLOTS * QUARTERS
VMEM_LIMIT = 42 * 1024 * 1024
PARTS = 4


def tile_of(j, q):
    return slice((j * QUARTERS + q) * LANE, (j * QUARTERS + q + 1) * LANE)


def replicated(per_choice):
    return jnp.concatenate([per_choice] * PER, axis=1)


def slot_members(ids, count):
    lanes = ids.shape[1]
    rows = lanes // PER
    expert = lax.broadcasted_iota(jnp.int32, (count, lanes), 0)
    chosen = [ids[k : k + 1, :] == expert for k in range(ids.shape[0])]
    present = functools.reduce(jnp.logical_or, chosen)
    first = lax.broadcasted_iota(jnp.int32, (lanes, lanes), 0)
    second = lax.broadcasted_iota(jnp.int32, (lanes, lanes), 1)
    before = jnp.logical_and(first // rows == second // rows, first < second).astype(bf16)
    earlier = jnp.dot(present.astype(bf16), before, preferred_element_type=f32)
    slot = (lax.broadcasted_iota(jnp.int32, (count, lanes), 1) // (rows * QUARTERS)).astype(f32)
    return jnp.logical_and(present, earlier == slot), chosen


def at_places(per_expert):
    count, lanes = per_expert.shape
    places = count * PER
    rows = lanes // PER
    place = lax.broadcasted_iota(jnp.int32, (places, count), 0)
    owner = lax.broadcasted_iota(jnp.int32, (places, count), 1)
    widen = (place // PER == owner).astype(bf16)
    wide = jnp.dot(widen, per_expert, preferred_element_type=f32)
    place = lax.broadcasted_iota(jnp.int32, (places, lanes), 0)
    lane = lax.broadcasted_iota(jnp.int32, (places, lanes), 1)
    return jnp.where(place % PER == lane // rows, wide, 0.0)


def pack_kernel(choices, meta_hbm, rows_hbm, send_ref, meta, rows, meta_sem, rows_sem):
    meta_copy = pltpu.make_async_copy(meta_hbm, meta, meta_sem)
    rows_copy = pltpu.make_async_copy(rows_hbm, rows, rows_sem)
    meta_copy.start()
    rows_copy.start()
    width = send_ref.shape[1]
    count = send_ref.shape[0] // PER
    meta_copy.wait()
    members, _ = slot_members(replicated(meta[:choices, :]), count)
    pick = at_places(members.astype(bf16)).astype(bf16)
    rows_copy.wait()
    quarters = jnp.concatenate(
        [
            jnp.concatenate([rows[:, tile_of(j, q)] for j in range(width // LANE)], axis=1)
            for q in range(QUARTERS)
        ]
        * SLOTS,
        axis=0,
    )
    send_ref[...] = jnp.dot(pick, quarters, preferred_element_type=f32).astype(bf16)


def pack(meta, moe_in, choices, count):
    rows, model_width = moe_in.shape
    return pl.pallas_call(
        functools.partial(pack_kernel, choices),
        out_shape=jax.ShapeDtypeStruct((count * PER, model_width // QUARTERS), bf16),
        in_specs=[pl.BlockSpec(memory_space=pltpu.HBM)] * 2,
        out_specs=pl.BlockSpec(memory_space=pltpu.VMEM),
        scratch_shapes=[
            pltpu.VMEM(meta.shape, meta.dtype),
            pltpu.VMEM(moe_in.shape, moe_in.dtype),
            pltpu.SemaphoreType.DMA,
            pltpu.SemaphoreType.DMA,
        ],
        compiler_params=pltpu.CompilerParams(vmem_limit_bytes=16 * 1024 * 1024),
        name="pack_rows",
    )(meta, moe_in)


def coefficient_table(ids, weights, count):
    members, chosen = slot_members(replicated(ids), count)
    weights = replicated(weights)
    weight = functools.reduce(jnp.add, [jnp.where(c, weights[k : k + 1, :], 0.0) for k, c in enumerate(chosen)])
    weight = jnp.where(members, weight, 0.0)
    high = weight.astype(bf16)
    low = (weight - high.astype(f32)).astype(bf16)
    tables = []
    for part in (high, low):
        table = jnp.transpose(at_places(part))
        half = table.shape[0] // SLOTS
        tables.append((table[:half] + table[half:]).astype(bf16))
    return jnp.concatenate(tables, axis=0)


def combine_kernel(coeff_ref, back_ref, out_ref):
    rows = out_ref.shape[0]
    width = back_ref.shape[1]
    total = jnp.dot(coeff_ref[...], back_ref[...], preferred_element_type=f32)
    for q in range(QUARTERS):
        low = (QUARTERS + q) * rows
        value = total[q * rows : (q + 1) * rows] + total[low : low + rows]
        for j in range(width // LANE):
            out_ref[:, tile_of(j, q)] = value[:, j * LANE : (j + 1) * LANE].astype(bf16)


def combine(coeff, back):
    rows = coeff.shape[0] // (2 * QUARTERS)
    return pl.pallas_call(
        combine_kernel,
        out_shape=jax.ShapeDtypeStruct((rows, back.shape[1] * QUARTERS), bf16),
        in_specs=[pl.BlockSpec(memory_space=pltpu.VMEM)] * 2,
        out_specs=pl.BlockSpec(memory_space=pltpu.VMEM),
        compiler_params=pltpu.CompilerParams(vmem_limit_bytes=16 * 1024 * 1024),
        name="combine_rows",
    )(coeff, back)


def attend(queries, latent, rope, length):
    kv_width = latent.shape[1]
    scores = lax.dot_general(
        queries[:, :kv_width], latent, (((1,), (1,)), ((), ())), preferred_element_type=f32
    )
    scores = (scores + jnp.dot(queries[:, kv_width:], rope, preferred_element_type=f32)) * score_scale
    positions = lax.broadcasted_iota(jnp.int32, (1, latent.shape[0]), 1)
    scores = jnp.where(positions < length, scores, -jnp.inf)
    weights = jnp.exp(scores - jnp.max(scores, axis=1, keepdims=True))
    probs = (weights / jnp.sum(weights, axis=1, keepdims=True)).astype(bf16)
    return jnp.dot(probs, latent, preferred_element_type=f32).astype(bf16)


def expert_kernel(
    got_ref, meta_hbm, weights_hbm, queries_hbm, latent_hbm, rope_hbm, gate_hbm, up_hbm, down_hbm,
    send_ref, coeff_ref, attn_ref,
    meta, weights, queries, latent, rope, gate_buf, up_buf, down_buf, wide, rows, hidden, small_sems, sems,
):
    tiles, places, _ = wide.shape
    count = places // PER
    parts, _, part = gate_buf.shape
    chunk = QUARTERS * LANE

    def places_of(s, q):
        return pl.ds(s * QUARTERS + q, count, stride=PER)

    small = [
        pltpu.make_async_copy(source, target, small_sems.at[i])
        for i, (source, target) in enumerate(
            ((meta_hbm, meta), (weights_hbm, weights), (queries_hbm, queries), (rope_hbm, rope), (latent_hbm, latent))
        )
    ]
    pairs = []
    for h in range(parts):
        columns = pl.ds(h * part, part)
        pairs += [(gate_hbm.at[:, columns], gate_buf.at[h]), (up_hbm.at[:, columns], up_buf.at[h])]
    for j in range(tiles):
        pairs.append((down_hbm.at[:, pl.ds(j * chunk, chunk)], down_buf.at[j]))
    queue = [pltpu.make_async_copy(source, target, sems.at[i]) for i, (source, target) in enumerate(pairs)]
    first, second = queue[: 2 * parts], queue[2 * parts :]

    def start(copies):
        for copy in copies:
            copy.start()

    def wait(copies):
        for copy in copies:
            copy.wait()

    start(small + first)
    for j in range(tiles):
        wide[j] = got_ref[:, j * LANE : (j + 1) * LANE].astype(f32)
        for q in range(QUARTERS):
            for s in range(SLOTS):
                rows[s * count : (s + 1) * count, tile_of(j, q)] = wide[j, places_of(s, q), :].astype(bf16)

    wait(small)
    coeff_ref[...] = coefficient_table(meta[: weights.shape[0], :], weights[...], count)
    attn_ref[...] = attend(jnp.transpose(queries[...]), latent[...], rope[...], meta[weights.shape[0] : weights.shape[0] + 1, 0:1])

    wait(first)
    start(second)
    for h in range(parts):
        gate = jnp.dot(rows[...], gate_buf[h], preferred_element_type=f32)
        up = jnp.dot(rows[...], up_buf[h], preferred_element_type=f32)
        hidden[:, h * part : (h + 1) * part] = (gate / (1.0 + jnp.exp(-gate)) * up).astype(bf16)
    wait(second)
    for j in range(tiles):
        result = jnp.dot(hidden[...], down_buf[j], preferred_element_type=f32)
        for q in range(QUARTERS):
            for s in range(SLOTS):
                wide[j, places_of(s, q), :] = result[s * count : (s + 1) * count, q * LANE : (q + 1) * LANE]
        send_ref[:, j * LANE : (j + 1) * LANE] = wide[j].astype(bf16)


def experts(got, meta, route_weights, gate_one, up_one, down_one, queries, latent, rope):
    places, width = got.shape
    heads, kv_width = queries.shape[1], latent.shape[1]
    model_width, hidden_width = gate_one.shape
    batch = SLOTS * places // PER
    vmem = pl.BlockSpec(memory_space=pltpu.VMEM)
    hbm = pl.BlockSpec(memory_space=pltpu.HBM)
    return pl.pallas_call(
        expert_kernel,
        out_shape=[
            jax.ShapeDtypeStruct((places, width), bf16),
            jax.ShapeDtypeStruct((2 * QUARTERS * meta.shape[1], places), bf16),
            jax.ShapeDtypeStruct((heads, kv_width), bf16),
        ],
        in_specs=[vmem, hbm, hbm, hbm, hbm, hbm, hbm, hbm, hbm],
        out_specs=[vmem] * 3,
        scratch_shapes=[
            pltpu.VMEM(meta.shape, meta.dtype),
            pltpu.VMEM(route_weights.shape, route_weights.dtype),
            pltpu.VMEM(queries.shape, queries.dtype),
            pltpu.VMEM(latent.shape, latent.dtype),
            pltpu.VMEM(rope.shape, rope.dtype),
            pltpu.VMEM((PARTS, model_width, hidden_width // PARTS), bf16),
            pltpu.VMEM((PARTS, model_width, hidden_width // PARTS), bf16),
            pltpu.VMEM((width // LANE, hidden_width, QUARTERS * LANE), bf16),
            pltpu.VMEM((width // LANE, places, LANE), f32),
            pltpu.VMEM((batch, model_width), bf16),
            pltpu.VMEM((batch, hidden_width), bf16),
            pltpu.SemaphoreType.DMA((5,)),
            pltpu.SemaphoreType.DMA((2 * PARTS + width // LANE,)),
        ],
        compiler_params=pltpu.CompilerParams(vmem_limit_bytes=VMEM_LIMIT),
        name="experts_and_attention",
    )(got, meta, route_weights, queries, latent, rope, gate_one, up_one, down_one)


def exchange(places):
    return lax.all_to_all(places, axes, split_axis=0, concat_axis=0, tiled=True)


def local(moe_in, route_ids, route_weights, w_gate, w_up, w_down, queries, cache_latent, cache_rope, lengths):
    count = lax.axis_size("node") * lax.axis_size("local")
    choices = route_ids.shape[1]
    filled = jnp.broadcast_to(lengths[:, None], (choices, route_ids.shape[0]))
    meta = jnp.concatenate([route_ids.T, filled], axis=0)
    got = exchange(pack(meta, moe_in, choices, count))
    results, coeff, attn_out = experts(
        got, meta, route_weights.T, w_gate[0], w_up[0], w_down[0], queries[0].T, cache_latent[0], cache_rope[0]
    )
    return combine(coeff, exchange(results)), attn_out[None]


def solution(mesh):
    row, cube = P(axes, None), P(axes, None, None)
    return jax.shard_map(
        local,
        mesh=mesh,
        in_specs=(row, row, row, cube, cube, cube, cube, cube, cube, P(axes)),
        out_specs=(row, cube),
        check_vma=False,
    )
```

time: 122 us -> 88.3 us (0.72)
  blocking collectives: 39.1 us -> 70.4 us
  local copies, waits for them, and re-layouts: 29.9 us -> 1.62 us
  waiting for transfers between devices: 23.7 us -> 0 us
  matrix products: 20.7 us -> 0 us
  Pallas kernels: 0 us -> 14.8 us
  starting transfers between devices: 5.83 us -> 0 us
    all_to_all x1 -> x2, blocking collectives: 39.1 us -> 70.4 us  [exchange(): return lax.all_to_all(places, axes, split_axis=0, concat_axis=0, tiled=True)]
    all_to_all x1 -> x0, waiting for transfers between devices: 23.7 us -> none  [local(): lax.all_to_all(result, ('node', 'local'), split_axis=0, concat_axis=0, ti...]
    dot_general x6 -> x0, matrix products: 20.7 us -> none  [the longest x1 11.2 us: expert_block(): jnp.dot(hidden_act, down_one, preferred_element_type=jnp.float32)]
    reshape x6 -> x0, local copies, waits for them, and re-layouts: 19.6 us -> none  [the longest x1 4.95 us: expert_block(): rows_flat = block.reshape(-1, model_width)]
    pallas_call x0 -> x3, Pallas kernels: none -> 14.8 us  [the longest x1 12.3 us: experts(): pl.pallas_call(expert_kernel, out_shape=[jax.ShapeDtypeStruct((places, wi...]
    gather x2 -> x0, local copies, waits for them, and re-layouts: 6.71 us -> none  [the longest x1 3.76 us: local(): picked = returned.reshape(expert_count * capacity, model_width)[slot_of]]
    all_to_all x1 -> x0, starting transfers between devices: 5.83 us -> none  [local(): lax.all_to_all(result, ('node', 'local'), split_axis=0, concat_axis=0, ti...]
  transfers between devices with their start and end apart: 1 -> 0, of which waited for: 1 -> 0; matrix products, arithmetic and copies ran while one was open for 2% -> 0% of each run, Pallas kernels for 0% -> 0%
where the time goes in v1:
time: 88.3 us; the launch traced here: 88.1 us
  blocking collectives  70.4 us (80%)
  Pallas kernels  14.8 us (17%)
  local copies, waits for them, and re-layouts  1.62 us (2%)
  between operations  1.34 us (2%)
    all_to_all x2, blocking collectives, exchange(): return lax.all_to_all(places, axes, split_axis=0, concat_axis=0, tiled=True)  70.4 us
    pallas_call x1, Pallas kernels, experts(): pl.pallas_call(expert_kernel, out_shape=[jax.ShapeDtypeStruct((places, wi...  12.3 us

profile of v1, /device:TPU:1, one launch (start us, length us, event | category | flops | bytes accessed | tf_op | source)
XLA Modules:
  0.0 88.1 jit_solution(2756794385307640004)
XLA Ops:
  1.3 0.7 concatenate.3.meta_hbm
  2.0 0.0 copy-start.3
  2.0 0.9 %copy-done.3 = bf16[16,3584]{1,0:T(8,128)(2,1)S(1)} copy-done((bf16[16,3584]{1,0:T(8,128)(2,1)S(1)}, bf16[16,3584]{1,0:T(8,128)(2,1)}, u32[]{:S(2)}) %copy-start.3) | copy-done | bytes 114712
  2.9 1.4 %pack_rows.1 = bf16[1024,896]{1,0:T(8,128)(2,1)S(1)} custom-call(s32[16,16]{1,0:T(8,128)S(1)} %concatenate.3.meta_hbm, bf16[16,3584]{1,0:T(8,128)(2,1)S(1)} %copy-done.3), custom_call_target="tpu_custom_call" | custom-call | tf_op jit(solution)/shard_map/pack_rows/pallas_call | solution.py:79
  4.2 0.0 copy-start
  4.2 0.0 copy-start.1
  4.3 0.0 copy-start.2
  4.3 0.0 copy-start.4
  4.3 38.8 %all_to_all.22 = bf16[128,8,896]{2,1,0:T(8,128)(2,1)S(1)} all-to-all(bf16[128,8,896]{2,1,0:T(8,128)(2,1)S(1)} %bitcast.19), channel_id=1, replica_groups=mesh['node'=16,'local'=8] {'node','local'}, dimensions={0} | all-to-all | bytes 3670016 | tf_op jit(solution)/shard_map/all_to_all | solution.py:245
  43.0 0.0 copy-done
  43.0 0.0 copy-done.1
  43.0 0.0 copy-done.2
  43.1 0.0 copy-done.4
  43.1 12.3 %experts_and_attention.1 = (bf16[1024,896]{1,0:T(8,128)(2,1)S(1)}, bf16[128,1024]{1,0:T(8,128)(2,1)S(1)}, bf16[128,512]{1,0:T(8,128)(2,1)}) custom-call(bf16[1024,896]{1,0:T(8,128)(2,1)S(1)} %bitcast.17, s32[16,16]{1,0:T(8,128)S(1)} %concatenate.3.meta_hbm, f32[8,16]{1,0:T(8,128)S(1)} %bitcast.24, bf16[576,128]{1,0:T(8,128)(2,1)S(1)} %bitcast.23, ...), custom_call_target="tpu_custom_call" | custom-call | tf_op jit(solution)/shard_map/experts_and_attention/pallas_call | solution.py:215
  55.4 31.6 %all_to_all.23 = bf16[128,8,896]{2,1,0:T(8,128)(2,1)S(1)} all-to-all(bf16[128,8,896]{2,1,0:T(8,128)(2,1)S(1)} %bitcast.21), channel_id=1, replica_groups=mesh['node'=16,'local'=8] {'node','local'}, dimensions={0} | all-to-all | bytes 3670016 | tf_op jit(solution)/shard_map/all_to_all | solution.py:245
  87.0 1.1 %combine_rows.1 = bf16[16,3584]{1,0:T(8,128)(2,1)} custom-call(bf16[128,1024]{1,0:T(8,128)(2,1)S(1)} %get-tuple-element.5.coeff_ref, bf16[1024,896]{1,0:T(8,128)(2,1)S(1)} %bitcast.18), custom_call_target="tpu_custom_call" | custom-call | tf_op jit(solution)/shard_map/combine_rows/pallas_call | solution.py:123
Async XLA Ops:
  2.0 0.9 %copy-start.3 = (bf16[16,3584]{1,0:T(8,128)(2,1)S(1)}, bf16[16,3584]{1,0:T(8,128)(2,1)}, u32[]{:S(2)}) copy-start(bf16[16,3584]{1,0:T(8,128)(2,1)} %rows_hbm.1) | copy-start | bytes 344068
  4.2 38.8 %copy-start = (bf16[1,2048,512]{2,1,0:T(8,128)(2,1)S(1)}, bf16[1,2048,512]{2,1,0:T(8,128)(2,1)}, u32[]{:S(2)}) copy-start(bf16[1,2048,512]{2,1,0:T(8,128)(2,1)} %param.17) | copy-start | bytes 6291460
  4.2 38.8 %copy-start.1 = (bf16[1,64,2048]{2,1,0:T(8,128)(2,1)S(1)}, bf16[1,64,2048]{2,1,0:T(8,128)(2,1)}, u32[]{:S(2)}) copy-start(bf16[1,64,2048]{2,1,0:T(8,128)(2,1)} %param.18) | copy-start | bytes 786436
  4.3 38.8 %copy-start.2 = (bf16[1,128,576]{1,2,0:T(8,128)(2,1)S(1)}, bf16[1,128,576]{1,2,0:T(8,128)(2,1)}, u32[]{:S(2)}) copy-start(bf16[1,128,576]{1,2,0:T(8,128)(2,1)} %param.16) | copy-start | bytes 442372
  4.3 38.8 %copy-start.4 = (f32[16,8]{0,1:T(8,128)S(1)}, f32[16,8]{0,1:T(8,128)}, u32[]{:S(2)}) copy-start(f32[16,8]{0,1:T(8,128)} %param.12) | copy-start | bytes 1540

commit v2 on v1

--- a/solution.py
+++ b/solution.py
@@ -13,7 +13,7 @@
 QUARTERS = 4
 LANE = 128
 PER = SLOTS * QUARTERS
-VMEM_LIMIT = 42 * 1024 * 1024
+VMEM_LIMIT = 33 * 1024 * 1024
 PARTS = 4
 
 
@@ -88,6 +88,7 @@
             pltpu.SemaphoreType.DMA,
         ],
         compiler_params=pltpu.CompilerParams(vmem_limit_bytes=16 * 1024 * 1024),
+        cost_estimate=pl.CostEstimate(flops=1 << 36, bytes_accessed=256 << 20, transcendentals=0),
         name="pack_rows",
     )(meta, moe_in)
 
@@ -144,13 +145,13 @@
 
 
 def expert_kernel(
-    got_ref, meta_hbm, weights_hbm, queries_hbm, latent_hbm, rope_hbm, gate_hbm, up_hbm, down_hbm,
+    got_ref, meta_hbm, weights_hbm, queries_hbm, latent_hbm, rope_hbm, gate_ref, up_ref, down_hbm,
     send_ref, coeff_ref, attn_ref,
-    meta, weights, queries, latent, rope, gate_buf, up_buf, down_buf, wide, rows, hidden, small_sems, sems,
+    meta, weights, queries, latent, rope, down_buf, wide, rows, hidden, small_sems, sems,
 ):
     tiles, places, _ = wide.shape
     count = places // PER
-    parts, _, part = gate_buf.shape
+    part = hidden.shape[1] // PARTS
     chunk = QUARTERS * LANE
 
     def places_of(s, q):
@@ -162,14 +163,9 @@
             ((meta_hbm, meta), (weights_hbm, weights), (queries_hbm, queries), (rope_hbm, rope), (latent_hbm, latent))
         )
     ]
-    pairs = []
-    for h in range(parts):
-        columns = pl.ds(h * part, part)
-        pairs += [(gate_hbm.at[:, columns], gate_buf.at[h]), (up_hbm.at[:, columns], up_buf.at[h])]
-    for j in range(tiles):
-        pairs.append((down_hbm.at[:, pl.ds(j * chunk, chunk)], down_buf.at[j]))
-    queue = [pltpu.make_async_copy(source, target, sems.at[i]) for i, (source, target) in enumerate(pairs)]
-    first, second = queue[: 2 * parts], queue[2 * parts :]
+    downs = [
+        pltpu.make_async_copy(down_hbm.at[:, pl.ds(j * chunk, chunk)], down_buf.at[j], sems.at[j]) for j in range(tiles)
+    ]
 
     def start(copies):
         for copy in copies:
@@ -179,24 +175,22 @@
         for copy in copies:
             copy.wait()
 
-    start(small + first)
+    start(small + downs)
+    wait(small)
+    coeff_ref[...] = coefficient_table(meta[: weights.shape[0], :], weights[...], count)
+    attn_ref[...] = attend(jnp.transpose(queries[...]), latent[...], rope[...], meta[weights.shape[0] : weights.shape[0] + 1, 0:1])
     for j in range(tiles):
         wide[j] = got_ref[:, j * LANE : (j + 1) * LANE].astype(f32)
         for q in range(QUARTERS):
             for s in range(SLOTS):
                 rows[s * count : (s + 1) * count, tile_of(j, q)] = wide[j, places_of(s, q), :].astype(bf16)
 
-    wait(small)
-    coeff_ref[...] = coefficient_table(meta[: weights.shape[0], :], weights[...], count)
-    attn_ref[...] = attend(jnp.transpose(queries[...]), latent[...], rope[...], meta[weights.shape[0] : weights.shape[0] + 1, 0:1])
-
-    wait(first)
-    start(second)
-    for h in range(parts):
-        gate = jnp.dot(rows[...], gate_buf[h], preferred_element_type=f32)
-        up = jnp.dot(rows[...], up_buf[h], preferred_element_type=f32)
-        hidden[:, h * part : (h + 1) * part] = (gate / (1.0 + jnp.exp(-gate)) * up).astype(bf16)
-    wait(second)
+    for h in range(PARTS):
+        columns = slice(h * part, (h + 1) * part)
+        gate = jnp.dot(rows[...], gate_ref[:, columns], preferred_element_type=f32)
+        up = jnp.dot(rows[...], up_ref[:, columns], preferred_element_type=f32)
+        hidden[:, columns] = (gate / (1.0 + jnp.exp(-gate)) * up).astype(bf16)
+    wait(downs)
     for j in range(tiles):
         result = jnp.dot(hidden[...], down_buf[j], preferred_element_type=f32)
         for q in range(QUARTERS):
@@ -219,7 +213,7 @@
             jax.ShapeDtypeStruct((2 * QUARTERS * meta.shape[1], places), bf16),
             jax.ShapeDtypeStruct((heads, kv_width), bf16),
         ],
-        in_specs=[vmem, hbm, hbm, hbm, hbm, hbm, hbm, hbm, hbm],
+        in_specs=[vmem, hbm, hbm, hbm, hbm, hbm, vmem, vmem, hbm],
         out_specs=[vmem] * 3,
         scratch_shapes=[
             pltpu.VMEM(meta.shape, meta.dtype),
@@ -227,14 +221,12 @@
             pltpu.VMEM(queries.shape, queries.dtype),
             pltpu.VMEM(latent.shape, latent.dtype),
             pltpu.VMEM(rope.shape, rope.dtype),
-            pltpu.VMEM((PARTS, model_width, hidden_width // PARTS), bf16),
-            pltpu.VMEM((PARTS, model_width, hidden_width // PARTS), bf16),
             pltpu.VMEM((width // LANE, hidden_width, QUARTERS * LANE), bf16),
             pltpu.VMEM((width // LANE, places, LANE), f32),
             pltpu.VMEM((batch, model_width), bf16),
             pltpu.VMEM((batch, hidden_width), bf16),
             pltpu.SemaphoreType.DMA((5,)),
-            pltpu.SemaphoreType.DMA((2 * PARTS + width // LANE,)),
+            pltpu.SemaphoreType.DMA((width // LANE,)),
         ],
         compiler_params=pltpu.CompilerParams(vmem_limit_bytes=VMEM_LIMIT),
         name="experts_and_attention",

time: 88.3 us -> 86.1 us (0.975)
  Pallas kernels: 14.8 us -> 11.9 us
    pallas_call x1, Pallas kernels: 12.3 us -> 9.44 us  [experts(): pl.pallas_call(expert_kernel, out_shape=[jax.ShapeDtypeStruct((places, wi...]
where the time goes in v2:
time: 86.1 us; the launch traced here: 85.9 us
  blocking collectives  70.4 us (82%)
  Pallas kernels  11.9 us (14%)
  local copies, waits for them, and re-layouts  2.22 us (3%)
  between operations  1.4 us (2%)
    all_to_all x2, blocking collectives, exchange(): return lax.all_to_all(places, axes, split_axis=0, concat_axis=0, tiled=True)  70.4 us
    pallas_call x1, Pallas kernels, experts(): pl.pallas_call(expert_kernel, out_shape=[jax.ShapeDtypeStruct((places, wi...  9.44 us

profile of v2, /device:TPU:1, one launch (start us, length us, event | category | flops | bytes accessed | tf_op | source)
XLA Modules:
  0.0 85.9 jit_solution(18185605826353348307)
XLA Ops:
  1.3 0.0 slice-start
  1.3 0.0 slice-start.2
  1.3 0.8 concatenate.3.meta_hbm
  2.1 0.0 copy-start.4
  2.1 1.3 %copy-done.4 = bf16[16,3584]{1,0:T(8,128)(2,1)S(1)} copy-done((bf16[16,3584]{1,0:T(8,128)(2,1)S(1)}, bf16[16,3584]{1,0:T(8,128)(2,1)}, u32[]{:S(2)}) %copy-start.4) | copy-done | bytes 114712
  3.5 0.0 slice-start.1
  3.5 0.0 slice-start.3
  3.5 1.4 %pack_rows.1 = bf16[1024,896]{1,0:T(8,128)(2,1)S(1)} custom-call(s32[16,16]{1,0:T(8,128)S(1)} %concatenate.3.meta_hbm, bf16[16,3584]{1,0:T(8,128)(2,1)S(1)} %copy-done.4), custom_call_target="tpu_custom_call" | custom-call | flops 68719476736 | bytes 268435456 | tf_op jit(solution)/shard_map/pack_rows/pallas_call | solution.py:79
  4.9 0.0 copy-start
  4.9 0.0 copy-start.1
  4.9 0.0 copy-start.2
  4.9 0.0 copy-start.3
  4.9 38.8 %all_to_all.22 = bf16[128,8,896]{2,1,0:T(8,128)(2,1)S(1)} all-to-all(bf16[128,8,896]{2,1,0:T(8,128)(2,1)S(1)} %bitcast.27), channel_id=1, replica_groups=mesh['node'=16,'local'=8] {'node','local'}, dimensions={0} | all-to-all | bytes 3670016 | tf_op jit(solution)/shard_map/all_to_all | solution.py:237
  43.7 0.0 slice-done
  43.7 0.0 slice-done.2
  43.7 0.0 slice-done.1
  43.7 0.0 slice-done.3
  43.7 0.0 copy-done
  43.7 0.0 copy-done.1
  43.7 0.0 copy-done.2
  43.7 0.0 copy-done.3
  43.8 9.4 %experts_and_attention.1 = (bf16[1024,896]{1,0:T(8,128)(2,1)S(1)}, bf16[128,1024]{1,0:T(8,128)(2,1)S(1)}, bf16[128,512]{1,0:T(8,128)(2,1)}) custom-call(bf16[1024,896]{1,0:T(8,128)(2,1)S(1)} %bitcast.17, s32[16,16]{1,0:T(8,128)S(1)} %concatenate.3.meta_hbm, f32[8,16]{1,0:T(8,128)S(1)} %bitcast.30, bf16[576,128]{1,0:T(8,128)(2,1)S(1)} %bitcast.29, ...), custom_call_target="tpu_custom_call" | custom-call | tf_op jit(solution)/shard_map/experts_and_attention/pallas_call | solution.py:209
  53.2 31.6 %all_to_all.23 = bf16[128,8,896]{2,1,0:T(8,128)(2,1)S(1)} all-to-all(bf16[128,8,896]{2,1,0:T(8,128)(2,1)S(1)} %bitcast.26), channel_id=1, replica_groups=mesh['node'=16,'local'=8] {'node','local'}, dimensions={0} | all-to-all | bytes 3670016 | tf_op jit(solution)/shard_map/all_to_all | solution.py:237
  84.8 1.1 %combine_rows.1 = bf16[16,3584]{1,0:T(8,128)(2,1)} custom-call(bf16[128,1024]{1,0:T(8,128)(2,1)S(1)} %get-tuple-element.5.coeff_ref, bf16[1024,896]{1,0:T(8,128)(2,1)S(1)} %bitcast.18), custom_call_target="tpu_custom_call" | custom-call | tf_op jit(solution)/shard_map/combine_rows/pallas_call | solution.py:124
  (2 shorter events, 0.0 us)
Async XLA Ops:
  1.3 42.4 %slice-start = ((s8[7340032]{0:T(1024)(128)(4,1)}), s8[4194304]{0:T(1024)(128)(4,1)S(1)}, s32[]{:S(2)}) async-start(s8[7340032]{0:T(1024)(128)(4,1)} %bitcast.19), calls=%async_computation.2 | async-start | bytes 8388608
  1.3 42.4 %slice-start.2 = ((s8[7340032]{0:T(1024)(128)(4,1)}), s8[4194304]{0:T(1024)(128)(4,1)S(1)}, s32[]{:S(2)}) async-start(s8[7340032]{0:T(1024)(128)(4,1)} %bitcast.22), calls=%async_computation.4 | async-start | bytes 8388608
  2.1 1.3 %copy-start.4 = (bf16[16,3584]{1,0:T(8,128)(2,1)S(1)}, bf16[16,3584]{1,0:T(8,128)(2,1)}, u32[]{:S(2)}) copy-start(bf16[16,3584]{1,0:T(8,128)(2,1)} %rows_hbm.1) | copy-start | bytes 344068
  3.5 40.2 %slice-start.1 = ((s8[7340032]{0:T(1024)(128)(4,1)}), s8[3145728]{0:T(1024)(128)(4,1)S(1)}, s32[]{:S(2)}) async-start(s8[7340032]{0:T(1024)(128)(4,1)} %bitcast.19), calls=%async_computation.3 | async-start | bytes 6291456
  3.5 40.2 %slice-start.3 = ((s8[7340032]{0:T(1024)(128)(4,1)}), s8[3145728]{0:T(1024)(128)(4,1)S(1)}, s32[]{:S(2)}) async-start(s8[7340032]{0:T(1024)(128)(4,1)} %bitcast.22), calls=%async_computation.5 | async-start | bytes 6291456
  4.9 38.8 %copy-start = (bf16[1,2048,512]{2,1,0:T(8,128)(2,1)S(1)}, bf16[1,2048,512]{2,1,0:T(8,128)(2,1)}, u32[]{:S(2)}) copy-start(bf16[1,2048,512]{2,1,0:T(8,128)(2,1)} %param.17) | copy-start | bytes 6291460
  4.9 38.8 %copy-start.1 = (bf16[1,64,2048]{2,1,0:T(8,128)(2,1)S(1)}, bf16[1,64,2048]{2,1,0:T(8,128)(2,1)}, u32[]{:S(2)}) copy-start(bf16[1,64,2048]{2,1,0:T(8,128)(2,1)} %param.18) | copy-start | bytes 786436
  4.9 38.8 %copy-start.2 = (bf16[1,128,576]{1,2,0:T(8,128)(2,1)S(1)}, bf16[1,128,576]{1,2,0:T(8,128)(2,1)}, u32[]{:S(2)}) copy-start(bf16[1,128,576]{1,2,0:T(8,128)(2,1)} %param.16) | copy-start | bytes 442372
  4.9 38.8 %copy-start.3 = (f32[16,8]{0,1:T(8,128)S(1)}, f32[16,8]{0,1:T(8,128)}, u32[]{:S(2)}) copy-start(f32[16,8]{0,1:T(8,128)} %param.12) | copy-start | bytes 1540

commit v3 on v2

--- a/solution.py
+++ b/solution.py
@@ -8,13 +8,15 @@
 
 f32, bf16 = jnp.float32, jnp.bfloat16
 score_scale = 192.0 ** (-0.5)
+LOG2_E = 1.4426950408889634
 axes = ("node", "local")
 SLOTS = 2
 QUARTERS = 4
 LANE = 128
 PER = SLOTS * QUARTERS
 VMEM_LIMIT = 33 * 1024 * 1024
-PARTS = 4
+PARTS = 2
+UNIT = 64
 
 
 def tile_of(j, q):
@@ -52,20 +54,23 @@
     return jnp.where(place % PER == lane // rows, wide, 0.0)
 
 
-def pack_kernel(choices, meta_hbm, rows_hbm, send_ref, meta, rows, meta_sem, rows_sem):
-    meta_copy = pltpu.make_async_copy(meta_hbm, meta, meta_sem)
-    rows_copy = pltpu.make_async_copy(rows_hbm, rows, rows_sem)
-    meta_copy.start()
-    rows_copy.start()
+def facts_of(meta, choices, rows):
+    start = meta.shape[0] - 2 * choices
+    values = meta[start:, :LANE].astype(f32)
+    length = values[choices : choices + 1, 0:1] * UNIT + values[2 * choices - 1 :, 0:1]
+    return values[:choices, :rows].astype(jnp.int32), length.astype(jnp.int32)
+
+
+def pack_kernel(choices, meta_ref, send_ref):
     width = send_ref.shape[1]
     count = send_ref.shape[0] // PER
-    meta_copy.wait()
-    members, _ = slot_members(replicated(meta[:choices, :]), count)
+    rows = meta_ref.shape[0] - 2 * choices
+    ids, _ = facts_of(meta_ref, choices, rows)
+    members, _ = slot_members(replicated(ids), count)
     pick = at_places(members.astype(bf16)).astype(bf16)
-    rows_copy.wait()
     quarters = jnp.concatenate(
         [
-            jnp.concatenate([rows[:, tile_of(j, q)] for j in range(width // LANE)], axis=1)
+            jnp.concatenate([meta_ref[:rows, tile_of(j, q)] for j in range(width // LANE)], axis=1)
             for q in range(QUARTERS)
         ]
         * SLOTS,
@@ -74,23 +79,16 @@
     send_ref[...] = jnp.dot(pick, quarters, preferred_element_type=f32).astype(bf16)
 
 
-def pack(meta, moe_in, choices, count):
-    rows, model_width = moe_in.shape
+def pack(meta, rows, choices, count):
     return pl.pallas_call(
         functools.partial(pack_kernel, choices),
-        out_shape=jax.ShapeDtypeStruct((count * PER, model_width // QUARTERS), bf16),
-        in_specs=[pl.BlockSpec(memory_space=pltpu.HBM)] * 2,
+        out_shape=jax.ShapeDtypeStruct((count * PER, meta.shape[1] // QUARTERS), bf16),
+        in_specs=[pl.BlockSpec(memory_space=pltpu.VMEM)],
         out_specs=pl.BlockSpec(memory_space=pltpu.VMEM),
-        scratch_shapes=[
-            pltpu.VMEM(meta.shape, meta.dtype),
-            pltpu.VMEM(moe_in.shape, moe_in.dtype),
-            pltpu.SemaphoreType.DMA,
-            pltpu.SemaphoreType.DMA,
-        ],
         compiler_params=pltpu.CompilerParams(vmem_limit_bytes=16 * 1024 * 1024),
         cost_estimate=pl.CostEstimate(flops=1 << 36, bytes_accessed=256 << 20, transcendentals=0),
         name="pack_rows",
-    )(meta, moe_in)
+    )(meta)
 
 
 def coefficient_table(ids, weights, count):
@@ -136,18 +134,18 @@
     scores = lax.dot_general(
         queries[:, :kv_width], latent, (((1,), (1,)), ((), ())), preferred_element_type=f32
     )
-    scores = (scores + jnp.dot(queries[:, kv_width:], rope, preferred_element_type=f32)) * score_scale
+    scores = scores + jnp.dot(queries[:, kv_width:], rope, preferred_element_type=f32)
     positions = lax.broadcasted_iota(jnp.int32, (1, latent.shape[0]), 1)
     scores = jnp.where(positions < length, scores, -jnp.inf)
-    weights = jnp.exp(scores - jnp.max(scores, axis=1, keepdims=True))
-    probs = (weights / jnp.sum(weights, axis=1, keepdims=True)).astype(bf16)
-    return jnp.dot(probs, latent, preferred_element_type=f32).astype(bf16)
+    weights = jnp.exp2((scores - jnp.max(scores, axis=1, keepdims=True)) * (score_scale * LOG2_E))
+    total = jnp.sum(weights, axis=1, keepdims=True)
+    return (jnp.dot(weights.astype(bf16), latent, preferred_element_type=f32) / total).astype(bf16)
 
 
 def expert_kernel(
-    got_ref, meta_hbm, weights_hbm, queries_hbm, latent_hbm, rope_hbm, gate_ref, up_ref, down_hbm,
+    got_ref, meta_ref, weights_hbm, queries_hbm, latent_hbm, rope_hbm, gate_ref, up_ref, down_hbm,
     send_ref, coeff_ref, attn_ref,
-    meta, weights, queries, latent, rope, down_buf, wide, rows, hidden, small_sems, sems,
+    weights, queries, latent, rope, down_buf, wide, rows, hidden, small_sems, sems,
 ):
     tiles, places, _ = wide.shape
     count = places // PER
@@ -160,7 +158,7 @@
     small = [
         pltpu.make_async_copy(source, target, small_sems.at[i])
         for i, (source, target) in enumerate(
-            ((meta_hbm, meta), (weights_hbm, weights), (queries_hbm, queries), (rope_hbm, rope), (latent_hbm, latent))
+            ((weights_hbm, weights), (queries_hbm, queries), (rope_hbm, rope), (latent_hbm, latent))
         )
     ]
     downs = [
@@ -177,8 +175,9 @@
 
     start(small + downs)
     wait(small)
-    coeff_ref[...] = coefficient_table(meta[: weights.shape[0], :], weights[...], count)
-    attn_ref[...] = attend(jnp.transpose(queries[...]), latent[...], rope[...], meta[weights.shape[0] : weights.shape[0] + 1, 0:1])
+    ids, length = facts_of(meta_ref, *weights.shape)
+    coeff_ref[...] = coefficient_table(ids, weights[...], count)
+    attn_ref[...] = attend(jnp.transpose(queries[...]), latent[...], rope[...], length)
     for j in range(tiles):
         wide[j] = got_ref[:, j * LANE : (j + 1) * LANE].astype(f32)
         for q in range(QUARTERS):
@@ -189,7 +188,7 @@
         columns = slice(h * part, (h + 1) * part)
         gate = jnp.dot(rows[...], gate_ref[:, columns], preferred_element_type=f32)
         up = jnp.dot(rows[...], up_ref[:, columns], preferred_element_type=f32)
-        hidden[:, columns] = (gate / (1.0 + jnp.exp(-gate)) * up).astype(bf16)
+        hidden[:, columns] = (gate * (0.5 + 0.5 * jnp.tanh(0.5 * gate)) * up).astype(bf16)
     wait(downs)
     for j in range(tiles):
         result = jnp.dot(hidden[...], down_buf[j], preferred_element_type=f32)
@@ -210,13 +209,12 @@
         expert_kernel,
         out_shape=[
             jax.ShapeDtypeStruct((places, width), bf16),
-            jax.ShapeDtypeStruct((2 * QUARTERS * meta.shape[1], places), bf16),
+            jax.ShapeDtypeStruct((2 * QUARTERS * route_weights.shape[1], places), bf16),
             jax.ShapeDtypeStruct((heads, kv_width), bf16),
         ],
-        in_specs=[vmem, hbm, hbm, hbm, hbm, hbm, vmem, vmem, hbm],
+        in_specs=[vmem, vmem, hbm, hbm, hbm, hbm, vmem, vmem, hbm],
         out_specs=[vmem] * 3,
         scratch_shapes=[
-            pltpu.VMEM(meta.shape, meta.dtype),
             pltpu.VMEM(route_weights.shape, route_weights.dtype),
             pltpu.VMEM(queries.shape, queries.dtype),
             pltpu.VMEM(latent.shape, latent.dtype),
@@ -225,7 +223,7 @@
             pltpu.VMEM((width // LANE, places, LANE), f32),
             pltpu.VMEM((batch, model_width), bf16),
             pltpu.VMEM((batch, hidden_width), bf16),
-            pltpu.SemaphoreType.DMA((5,)),
+            pltpu.SemaphoreType.DMA((4,)),
             pltpu.SemaphoreType.DMA((width // LANE,)),
         ],
         compiler_params=pltpu.CompilerParams(vmem_limit_bytes=VMEM_LIMIT),
@@ -240,9 +238,15 @@
 def local(moe_in, route_ids, route_weights, w_gate, w_up, w_down, queries, cache_latent, cache_rope, lengths):
     count = lax.axis_size("node") * lax.axis_size("local")
     choices = route_ids.shape[1]
-    filled = jnp.broadcast_to(lengths[:, None], (choices, route_ids.shape[0]))
-    meta = jnp.concatenate([route_ids.T, filled], axis=0)
-    got = exchange(pack(meta, moe_in, choices, count))
+    rows, model_width = moe_in.shape
+    tail = (rows + 2 * choices, model_width)
+    row = lax.broadcasted_iota(jnp.int32, tail, 0)
+    length = lengths[0]
+    facts = jnp.pad(route_ids.T, ((rows, choices), (0, model_width - rows)))
+    filled = jnp.where(row < rows + choices + choices // 2, length // UNIT, length % UNIT)
+    meta = jnp.pad(moe_in, ((0, 2 * choices), (0, 0)))
+    meta = jnp.where(row < rows, meta, jnp.where(row < rows + choices, facts, filled).astype(bf16))
+    got = exchange(pack(meta, rows, choices, count))
     results, coeff, attn_out = experts(
         got, meta, route_weights.T, w_gate[0], w_up[0], w_down[0], queries[0].T, cache_latent[0], cache_rope[0]
     )

time: 86.1 us -> 84.5 us (0.981)
  local copies, waits for them, and re-layouts: 2.22 us -> 0.06 us
  other arithmetic: 0.01 us -> 1.17 us
    unnamed x18 -> x16, local copies, waits for them, and re-layouts: 1.38 us -> 0.06 us
    select_n x0 -> x2, other arithmetic: none -> 1.16 us  [the longest x1 1.16 us: local(): jnp.where(row < rows, meta, jnp.where(row < rows + choices, facts, filled...]
where the time goes in v3:
time: 84.5 us; the launch traced here: 84.3 us
  blocking collectives  70.4 us (83%)
  Pallas kernels  11.2 us (13%)
  between operations  1.48 us (2%)
  other arithmetic  1.17 us (1%)
    all_to_all x2, blocking collectives, exchange(): return lax.all_to_all(places, axes, split_axis=0, concat_axis=0, tiled=True)  70.4 us
    pallas_call x1, Pallas kernels, experts(): pl.pallas_call(expert_kernel, out_shape=[jax.ShapeDtypeStruct((places, wi...  9.08 us

profile of v3, /device:TPU:1, one launch (start us, length us, event | category | flops | bytes accessed | tf_op | source)
XLA Modules:
  0.0 84.3 jit_solution(341371869562755179)
XLA Ops:
  1.3 0.0 slice-start
  1.4 0.0 slice-start.2
  1.4 1.2 %fusion.meta_ref = bf16[32,3584]{1,0:T(8,128)(2,1)S(1)} fusion(s32[8,16]{1,0:T(8,128)} %bitcast.35, s32[32]{0:T(128)S(1)} %compare_select_fusion, bf16[16,3584]{1,0:T(8,128)(2,1)} %param.10, pred[32]{0:T(512)(128)(4,1)S(1)} %get-tuple-element.8, pred[32]{0:T(512)(128)(4,1)S(1)} %get-tuple-element.9), kind=kLoop, calls=%fused_computation.1 | loop fusion | flops 344064 | bytes 344768 | tf_op jit(solution)/shard_map/jit(_where)/select_n | solution.py:248
  2.5 0.0 slice-start.1
  2.6 0.0 slice-start.3
  2.6 1.0 %pack_rows.1 = bf16[1024,896]{1,0:T(8,128)(2,1)S(1)} custom-call(bf16[32,3584]{1,0:T(8,128)(2,1)S(1)} %fusion.meta_ref), custom_call_target="tpu_custom_call" | custom-call | flops 68719476736 | bytes 268435456 | tf_op jit(solution)/shard_map/pack_rows/pallas_call | solution.py:83
  3.6 0.0 copy-start
  3.6 0.0 copy-start.1
  3.6 0.0 copy-start.2
  3.6 0.0 copy-start.3
  3.7 38.8 %all_to_all.22 = bf16[128,8,896]{2,1,0:T(8,128)(2,1)S(1)} all-to-all(bf16[128,8,896]{2,1,0:T(8,128)(2,1)S(1)} %bitcast.30), channel_id=1, replica_groups=mesh['node'=16,'local'=8] {'node','local'}, dimensions={0} | all-to-all | bytes 3670016 | tf_op jit(solution)/shard_map/all_to_all | solution.py:235
  42.4 0.0 slice-done
  42.4 0.0 slice-done.2
  42.4 0.0 slice-done.1
  42.4 0.0 slice-done.3
  42.5 0.0 copy-done
  42.5 0.0 copy-done.1
  42.5 0.0 copy-done.2
  42.5 0.0 copy-done.3
  42.5 9.1 %experts_and_attention.1 = (bf16[1024,896]{1,0:T(8,128)(2,1)S(1)}, bf16[128,1024]{1,0:T(8,128)(2,1)S(1)}, bf16[128,512]{1,0:T(8,128)(2,1)}) custom-call(bf16[1024,896]{1,0:T(8,128)(2,1)S(1)} %bitcast.20, bf16[32,3584]{1,0:T(8,128)(2,1)S(1)} %fusion.meta_ref, f32[8,16]{1,0:T(8,128)S(1)} %bitcast.33, bf16[576,128]{1,0:T(8,128)(2,1)S(1)} %bitcast.32, ...), custom_call_target="tpu_custom_call" | custom-call | tf_op jit(solution)/shard_map/experts_and_attention/pallas_call | solution.py:208
  51.6 31.6 %all_to_all.23 = bf16[128,8,896]{2,1,0:T(8,128)(2,1)S(1)} all-to-all(bf16[128,8,896]{2,1,0:T(8,128)(2,1)S(1)} %bitcast.29), channel_id=1, replica_groups=mesh['node'=16,'local'=8] {'node','local'}, dimensions={0} | all-to-all | bytes 3670016 | tf_op jit(solution)/shard_map/all_to_all | solution.py:235
  83.2 1.1 %combine_rows.1 = bf16[16,3584]{1,0:T(8,128)(2,1)} custom-call(bf16[128,1024]{1,0:T(8,128)(2,1)S(1)} %get-tuple-element.5.coeff_ref, bf16[1024,896]{1,0:T(8,128)(2,1)S(1)} %bitcast.21), custom_call_target="tpu_custom_call" | custom-call | tf_op jit(solution)/shard_map/combine_rows/pallas_call | solution.py:122
  (4 shorter events, 0.0 us)
Async XLA Ops:
  1.3 41.1 %slice-start = ((s8[7340032]{0:T(1024)(128)(4,1)}), s8[4194304]{0:T(1024)(128)(4,1)S(1)}, s32[]{:S(2)}) async-start(s8[7340032]{0:T(1024)(128)(4,1)} %bitcast.22), calls=%async_computation.2 | async-start | bytes 8388608
  1.4 41.1 %slice-start.2 = ((s8[7340032]{0:T(1024)(128)(4,1)}), s8[4194304]{0:T(1024)(128)(4,1)S(1)}, s32[]{:S(2)}) async-start(s8[7340032]{0:T(1024)(128)(4,1)} %bitcast.25), calls=%async_computation.4 | async-start | bytes 8388608
  2.5 39.9 %slice-start.1 = ((s8[7340032]{0:T(1024)(128)(4,1)}), s8[3145728]{0:T(1024)(128)(4,1)S(1)}, s32[]{:S(2)}) async-start(s8[7340032]{0:T(1024)(128)(4,1)} %bitcast.22), calls=%async_computation.3 | async-start | bytes 6291456
  2.6 39.9 %slice-start.3 = ((s8[7340032]{0:T(1024)(128)(4,1)}), s8[3145728]{0:T(1024)(128)(4,1)S(1)}, s32[]{:S(2)}) async-start(s8[7340032]{0:T(1024)(128)(4,1)} %bitcast.25), calls=%async_computation.5 | async-start | bytes 6291456
  3.6 38.8 %copy-start = (bf16[1,2048,512]{2,1,0:T(8,128)(2,1)S(1)}, bf16[1,2048,512]{2,1,0:T(8,128)(2,1)}, u32[]{:S(2)}) copy-start(bf16[1,2048,512]{2,1,0:T(8,128)(2,1)} %param.17) | copy-start | bytes 6291460
  3.6 38.8 %copy-start.1 = (bf16[1,64,2048]{2,1,0:T(8,128)(2,1)S(1)}, bf16[1,64,2048]{2,1,0:T(8,128)(2,1)}, u32[]{:S(2)}) copy-start(bf16[1,64,2048]{2,1,0:T(8,128)(2,1)} %param.18) | copy-start | bytes 786436
  3.6 38.8 %copy-start.2 = (bf16[1,128,576]{1,2,0:T(8,128)(2,1)S(1)}, bf16[1,128,576]{1,2,0:T(8,128)(2,1)}, u32[]{:S(2)}) copy-start(bf16[1,128,576]{1,2,0:T(8,128)(2,1)} %param.16) | copy-start | bytes 442372
  3.6 38.8 %copy-start.3 = (f32[16,8]{0,1:T(8,128)S(1)}, f32[16,8]{0,1:T(8,128)}, u32[]{:S(2)}) copy-start(f32[16,8]{0,1:T(8,128)} %param.12) | copy-start | bytes 1540

commit v4 on v3

--- a/solution.py
+++ b/solution.py
@@ -17,6 +17,7 @@
 VMEM_LIMIT = 33 * 1024 * 1024
 PARTS = 2
 UNIT = 64
+GROUP = 1
 
 
 def tile_of(j, q):
@@ -161,9 +162,7 @@
             ((weights_hbm, weights), (queries_hbm, queries), (rope_hbm, rope), (latent_hbm, latent))
         )
     ]
-    downs = [
-        pltpu.make_async_copy(down_hbm.at[:, pl.ds(j * chunk, chunk)], down_buf.at[j], sems.at[j]) for j in range(tiles)
-    ]
+    downs = [pltpu.make_async_copy(down_hbm, down_buf, sems.at[0])]
 
     def start(copies):
         for copy in copies:
@@ -190,12 +189,15 @@
         up = jnp.dot(rows[...], up_ref[:, columns], preferred_element_type=f32)
         hidden[:, columns] = (gate * (0.5 + 0.5 * jnp.tanh(0.5 * gate)) * up).astype(bf16)
     wait(downs)
-    for j in range(tiles):
-        result = jnp.dot(hidden[...], down_buf[j], preferred_element_type=f32)
-        for q in range(QUARTERS):
-            for s in range(SLOTS):
-                wide[j, places_of(s, q), :] = result[s * count : (s + 1) * count, q * LANE : (q + 1) * LANE]
-        send_ref[:, j * LANE : (j + 1) * LANE] = wide[j].astype(bf16)
+    for first in range(0, tiles, GROUP):
+        last = min(first + GROUP, tiles)
+        result = jnp.dot(hidden[...], down_buf[:, first * chunk : last * chunk], preferred_element_type=f32)
+        for j in range(first, last):
+            for q in range(QUARTERS):
+                at = ((j - first) * QUARTERS + q) * LANE
+                for s in range(SLOTS):
+                    wide[j, places_of(s, q), :] = result[s * count : (s + 1) * count, at : at + LANE]
+            send_ref[:, j * LANE : (j + 1) * LANE] = wide[j].astype(bf16)
 
 
 def experts(got, meta, route_weights, gate_one, up_one, down_one, queries, latent, rope):
@@ -219,12 +221,12 @@
             pltpu.VMEM(queries.shape, queries.dtype),
             pltpu.VMEM(latent.shape, latent.dtype),
             pltpu.VMEM(rope.shape, rope.dtype),
-            pltpu.VMEM((width // LANE, hidden_width, QUARTERS * LANE), bf16),
+            pltpu.VMEM(down_one.shape, bf16),
             pltpu.VMEM((width // LANE, places, LANE), f32),
             pltpu.VMEM((batch, model_width), bf16),
             pltpu.VMEM((batch, hidden_width), bf16),
             pltpu.SemaphoreType.DMA((4,)),
-            pltpu.SemaphoreType.DMA((width // LANE,)),
+            pltpu.SemaphoreType.DMA((1,)),
         ],
         compiler_params=pltpu.CompilerParams(vmem_limit_bytes=VMEM_LIMIT),
         name="experts_and_attention",
@@ -241,11 +243,12 @@
     rows, model_width = moe_in.shape
     tail = (rows + 2 * choices, model_width)
     row = lax.broadcasted_iota(jnp.int32, tail, 0)
-    length = lengths[0]
-    facts = jnp.pad(route_ids.T, ((rows, choices), (0, model_width - rows)))
-    filled = jnp.where(row < rows + choices + choices // 2, length // UNIT, length % UNIT)
+    ids = jnp.pad(route_ids.T, ((rows, choices), (0, model_width - rows)))
+    length = lengths[:, None]
+    units = jnp.pad(length // UNIT, ((rows + choices, choices - 1), (0, model_width - 1)))
+    rest = jnp.pad(length % UNIT, ((rows + 2 * choices - 1, 0), (0, model_width - 1)))
     meta = jnp.pad(moe_in, ((0, 2 * choices), (0, 0)))
-    meta = jnp.where(row < rows, meta, jnp.where(row < rows + choices, facts, filled).astype(bf16))
+    meta = jnp.where(row < rows, meta, (ids + units + rest).astype(bf16))
     got = exchange(pack(meta, rows, choices, count))
     results, coeff, attn_out = experts(
         got, meta, route_weights.T, w_gate[0], w_up[0], w_down[0], queries[0].T, cache_latent[0], cache_rope[0]

time: 84.5 us -> 84.4 us (level)
  no operation moved by 1% of the time
where the time goes in v4:
time: 84.4 us; the launch traced here: 84.2 us
  blocking collectives  70.4 us (83%)
  Pallas kernels  11.1 us (13%)
  between operations  1.47 us (2%)
  other arithmetic  1.16 us (1%)
    all_to_all x2, blocking collectives, exchange(): return lax.all_to_all(places, axes, split_axis=0, concat_axis=0, tiled=True)  70.4 us
    pallas_call x1, Pallas kernels, experts(): pl.pallas_call(expert_kernel, out_shape=[jax.ShapeDtypeStruct((places, wi...  9 us

profile of v4, /device:TPU:1, one launch (start us, length us, event | category | flops | bytes accessed | tf_op | source)
XLA Modules:
  0.0 84.2 jit_solution(2326464080434845898)
XLA Ops:
  1.3 0.0 slice-start
  1.3 0.0 slice-start.2
  1.4 1.2 %fusion.meta_ref = bf16[32,3584]{1,0:T(8,128)(2,1)S(1)} fusion(s32[1,1]{1,0:T(1,128)S(6)} %select_n.17, s32[1,1]{1,0:T(1,128)S(6)} %select_n.16, s32[8,16]{1,0:T(8,128)} %bitcast.35, bf16[16,3584]{1,0:T(8,128)(2,1)} %param.10, pred[32]{0:T(512)(128)(4,1)S(1)} %iota_compare_fusion), kind=kLoop, calls=%fused_computation.1 | loop fusion | flops 458752 | bytes 344616 | tf_op jit(solution)/shard_map/jit(_where)/select_n | solution.py:251
  2.5 0.0 slice-start.1
  2.5 0.0 slice-start.3
  2.5 1.0 %pack_rows.1 = bf16[1024,896]{1,0:T(8,128)(2,1)S(1)} custom-call(bf16[32,3584]{1,0:T(8,128)(2,1)S(1)} %fusion.meta_ref), custom_call_target="tpu_custom_call" | custom-call | flops 68719476736 | bytes 268435456 | tf_op jit(solution)/shard_map/pack_rows/pallas_call | solution.py:84
  3.6 0.0 copy-start
  3.6 0.0 copy-start.1
  3.6 0.0 copy-start.2
  3.6 0.0 copy-start.3
  3.6 38.8 %all_to_all.22 = bf16[128,8,896]{2,1,0:T(8,128)(2,1)S(1)} all-to-all(bf16[128,8,896]{2,1,0:T(8,128)(2,1)S(1)} %bitcast.30), channel_id=1, replica_groups=mesh['node'=16,'local'=8] {'node','local'}, dimensions={0} | all-to-all | bytes 3670016 | tf_op jit(solution)/shard_map/all_to_all | solution.py:237
  42.4 0.0 slice-done
  42.4 0.0 slice-done.2
  42.4 0.0 slice-done.1
  42.4 0.0 slice-done.3
  42.4 0.0 copy-done
  42.4 0.0 copy-done.1
  42.5 0.0 copy-done.2
  42.5 0.0 copy-done.3
  42.5 9.0 %experts_and_attention.1 = (bf16[1024,896]{1,0:T(8,128)(2,1)S(1)}, bf16[128,1024]{1,0:T(8,128)(2,1)S(1)}, bf16[128,512]{1,0:T(8,128)(2,1)}) custom-call(bf16[1024,896]{1,0:T(8,128)(2,1)S(1)} %bitcast.20, bf16[32,3584]{1,0:T(8,128)(2,1)S(1)} %fusion.meta_ref, f32[8,16]{1,0:T(8,128)S(1)} %bitcast.33, bf16[576,128]{1,0:T(8,128)(2,1)S(1)} %bitcast.32, ...), custom_call_target="tpu_custom_call" | custom-call | tf_op jit(solution)/shard_map/experts_and_attention/pallas_call | solution.py:210
  51.5 31.6 %all_to_all.23 = bf16[128,8,896]{2,1,0:T(8,128)(2,1)S(1)} all-to-all(bf16[128,8,896]{2,1,0:T(8,128)(2,1)S(1)} %bitcast.29), channel_id=1, replica_groups=mesh['node'=16,'local'=8] {'node','local'}, dimensions={0} | all-to-all | bytes 3670016 | tf_op jit(solution)/shard_map/all_to_all | solution.py:237
  83.1 1.1 %combine_rows.1 = bf16[16,3584]{1,0:T(8,128)(2,1)} custom-call(bf16[128,1024]{1,0:T(8,128)(2,1)S(1)} %get-tuple-element.5.coeff_ref, bf16[1024,896]{1,0:T(8,128)(2,1)S(1)} %bitcast.21), custom_call_target="tpu_custom_call" | custom-call | tf_op jit(solution)/shard_map/combine_rows/pallas_call | solution.py:123
  (3 shorter events, 0.0 us)
Async XLA Ops:
  1.3 41.1 %slice-start = ((s8[7340032]{0:T(1024)(128)(4,1)}), s8[4194304]{0:T(1024)(128)(4,1)S(1)}, s32[]{:S(2)}) async-start(s8[7340032]{0:T(1024)(128)(4,1)} %bitcast.22), calls=%async_computation.2 | async-start | bytes 8388608
  1.3 41.1 %slice-start.2 = ((s8[7340032]{0:T(1024)(128)(4,1)}), s8[4194304]{0:T(1024)(128)(4,1)S(1)}, s32[]{:S(2)}) async-start(s8[7340032]{0:T(1024)(128)(4,1)} %bitcast.25), calls=%async_computation.4 | async-start | bytes 8388608
  2.5 39.9 %slice-start.1 = ((s8[7340032]{0:T(1024)(128)(4,1)}), s8[3145728]{0:T(1024)(128)(4,1)S(1)}, s32[]{:S(2)}) async-start(s8[7340032]{0:T(1024)(128)(4,1)} %bitcast.22), calls=%async_computation.3 | async-start | bytes 6291456
  2.5 39.9 %slice-start.3 = ((s8[7340032]{0:T(1024)(128)(4,1)}), s8[3145728]{0:T(1024)(128)(4,1)S(1)}, s32[]{:S(2)}) async-start(s8[7340032]{0:T(1024)(128)(4,1)} %bitcast.25), calls=%async_computation.5 | async-start | bytes 6291456
  3.6 38.8 %copy-start = (bf16[1,2048,512]{2,1,0:T(8,128)(2,1)S(1)}, bf16[1,2048,512]{2,1,0:T(8,128)(2,1)}, u32[]{:S(2)}) copy-start(bf16[1,2048,512]{2,1,0:T(8,128)(2,1)} %param.17) | copy-start | bytes 6291460
  3.6 38.8 %copy-start.1 = (bf16[1,64,2048]{2,1,0:T(8,128)(2,1)S(1)}, bf16[1,64,2048]{2,1,0:T(8,128)(2,1)}, u32[]{:S(2)}) copy-start(bf16[1,64,2048]{2,1,0:T(8,128)(2,1)} %param.18) | copy-start | bytes 786436
  3.6 38.8 %copy-start.2 = (bf16[1,128,576]{1,2,0:T(8,128)(2,1)S(1)}, bf16[1,128,576]{1,2,0:T(8,128)(2,1)}, u32[]{:S(2)}) copy-start(bf16[1,128,576]{1,2,0:T(8,128)(2,1)} %param.16) | copy-start | bytes 442372
  3.6 38.8 %copy-start.3 = (f32[16,8]{0,1:T(8,128)S(1)}, f32[16,8]{0,1:T(8,128)}, u32[]{:S(2)}) copy-start(f32[16,8]{0,1:T(8,128)} %param.12) | copy-start | bytes 1540
